TPU v7x, 512 devices: a whole 4x8x8 slice. The times are simulated.
512 devices in a mesh: dp: 16 (over y, core), expert: 32 (over z, x).
Axes of the slice: x: 4, y: 8, z: 8, core: 2. Of those that a mesh axis runs over, the one named last changes fastest.
Arguments:
- stream_q: bfloat16 [4096, 4096], P('dp', 'expert'), may hold values from -6 to 6
- stream_k: bfloat16 [4096, 4096], P('dp', 'expert'), may hold values from -6 to 6
- stream_v: bfloat16 [4096, 4096], P('dp', 'expert'), may hold values from -6 to 6
- conv_taps: float32 [3, 3, 4096], P(None, None, 'expert'), may hold values from -14 to 14
- norm_gain: bfloat16 [4096], P('expert'), may hold values from 0.3984375 to 1.59375
- slot_token: int32 [16, 384], P('dp'), may hold values from 0 to 256, as said below
- expert_count: int32 [16, 2], P('dp'), may hold values from 0 to 256, as said below
- route_prob: float32 [4096], P('dp'), may hold values from 0.25 to 1
- w_proj: bfloat16 [4096, 2, 8192], P('dp', None, 'expert'), may hold values from -0.09375 to 0.09375
- grad_out: bfloat16 [4096, 8192], P('dp', 'expert'), may hold values from -0.75 to 0.75
Outputs:
- activation: bfloat16 [4096, 8192], P('dp', 'expert')
- weight_grad: float32 [4096, 2, 8192], P('dp', None, 'expert')
Inputs may be any that keep to these rules, and one draw needn't show every extreme that they name: `slot_token`: for each index of dp the slots hold its 256 local token numbers, each exactly once, grouped by expert in expert order; each group starts at a multiple of 128 and is padded with the value 256 up to a multiple of 128; all slots after the last group hold 256. `expert_count`: the size of each expert's group in slot_token, before padding; each row sums to 256.
All inputs are finite; a program needn't handle non-finite values.
Results may differ from a plain program's by a relative error of at most 0.023.
Values may be sent and summed in bfloat16 or wider, within the bound.
No kernel may reach another device: no remote copies, remote signals or barrier semaphores. Data moves between devices by JAX's collectives and lax.ppermute only.
A program may use at most 64 MiB of HBM per device.

v0:
```python
import jax
import jax.numpy as jnp
from jax import lax
from jax.sharding import PartitionSpec as P

D = 4096
BLOCK = 128
epsilon = 1e-06


def from_behind(value, axis, steps):
    count = lax.axis_size(axis)
    leading, last = (max(0, -steps), min(count, count - steps))
    return lax.ppermute(value, axis, [(source, source + steps) for source in range(leading, last)])


def block_owner(counts, num_blocks):
    padded = (counts + BLOCK - 1) // BLOCK * BLOCK
    ends = jnp.cumsum(padded)
    starts = jnp.arange(num_blocks, dtype=jnp.int32) * BLOCK
    owner = jnp.sum((starts[:, None] >= ends[None, :]).astype(jnp.int32), axis=1)
    return jnp.minimum(owner, counts.shape[0] - 1)


def on_device(
    stream_q,
    stream_k,
    stream_v,
    conv_taps,
    norm_gain,
    slot_token,
    expert_count,
    route_prob,
    w_proj,
    grad_out,
):
    stacked = jnp.stack([stream_q, stream_k, stream_v])
    before = from_behind(stacked[:, -2:, :], "dp", 1)
    extended = jnp.concatenate([before, stacked], axis=1).astype(jnp.float32)
    convolved = (
        conv_taps[:, 0, None, :] * extended[:, 2:]
        + conv_taps[:, 1, None, :] * extended[:, 1:-1]
        + conv_taps[:, 2, None, :] * extended[:, :-2]
    )
    mixed = (convolved[0] * convolved[1] * convolved[2]).astype(jnp.bfloat16)
    mixed_f = mixed.astype(jnp.float32)
    total = lax.psum(jnp.sum(mixed_f * mixed_f, axis=1), "expert")
    inv_rms = lax.rsqrt(total / D + epsilon)
    normed = (mixed_f * inv_rms[:, None] * norm_gain.astype(jnp.float32)).astype(jnp.bfloat16)
    gathered = lax.all_gather(normed, "expert", axis=1, tiled=True)
    tok_count = gathered.shape[0]
    slots = slot_token[0]
    num_blocks = slots.shape[0] // BLOCK
    owner = block_owner(expert_count[0], num_blocks)
    padded_rows = jnp.concatenate(
        [gathered, jnp.zeros((1, gathered.shape[1]), jnp.bfloat16)], axis=0
    )
    x_blocks = padded_rows[slots].reshape(num_blocks, BLOCK, gathered.shape[1])
    hid_local = w_proj.shape[2]
    experts_here = w_proj.shape[1]
    selector = (owner[:, None] == jnp.arange(experts_here, dtype=jnp.int32)[None, :]).astype(
        jnp.bfloat16
    )
    columns = x_blocks
    chosen_w = jnp.einsum(
        "neh,be->bnh",
        lax.all_gather(w_proj, "dp", axis=0, tiled=True),
        selector,
        preferred_element_type=jnp.float32,
    ).astype(jnp.bfloat16)
    pre_act = jnp.einsum("brn,bnh->brh", columns, chosen_w, preferred_element_type=jnp.float32)
    pre_act = pre_act.reshape(num_blocks * BLOCK, hid_local)
    slot_prob = jnp.concatenate([route_prob, jnp.zeros((1,), jnp.float32)])[slots][:, None]
    sigmoid_z = jax.nn.sigmoid(pre_act)
    hidden = (slot_prob * pre_act * sigmoid_z).astype(jnp.bfloat16)
    activation = (
        jnp.zeros((tok_count + 1, hid_local), jnp.bfloat16).at[slots].set(hidden)[:tok_count]
    )
    slot_grad = jnp.concatenate([grad_out, jnp.zeros((1, hid_local), jnp.bfloat16)], axis=0)[
        slots
    ].astype(jnp.float32)
    grad_pre = (slot_grad * slot_prob * sigmoid_z * (1.0 + pre_act * (1.0 - sigmoid_z))).astype(
        jnp.bfloat16
    )
    grad_blocks = grad_pre.reshape(num_blocks, BLOCK, hid_local)
    masked_grad = grad_blocks[None, :, :, :] * selector.T[:, :, None, None]
    columns = x_blocks
    weight_grad = lax.psum_scatter(
        jnp.einsum(
            "brd,ebrh->deh", columns, masked_grad, preferred_element_type=jnp.float32
        ).astype(jnp.bfloat16),
        "dp",
        scatter_dimension=0,
        tiled=True,
    ).astype(jnp.float32)
    return (activation, weight_grad)


def solution(mesh):
    placed = (
        P("dp", "expert"),
        P("dp", "expert"),
        P("dp", "expert"),
        P(None, None, "expert"),
        P("expert"),
        P("dp", None),
        P("dp", None),
        P("dp"),
        P("dp", None, "expert"),
        P("dp", "expert"),
    )
    return jax.shard_map(
        on_device,
        mesh=mesh,
        in_specs=placed,
        out_specs=(P("dp", "expert"), P("dp", None, "expert")),
        check_vma=False,
    )
```

profile of v0, /device:TPU:29, one launch (start us, length us, event | category | flops | bytes accessed | tf_op | source)
XLA Modules:
  0.0 303.6 jit_solution(1994741817525698117)
XLA Ops:
  7.2 0.0 copy-start.2
  7.2 0.0 copy-start.3
  7.2 0.0 all-gather.3.cloned.1.call-start
  7.2 0.7 pad_maximum_fusion.1
  8.0 5.0 %collective-permute-start = (bf16[3,2,128]{2,1,0:T(2,128)(2,1)S(1)}, bf16[3,2,128]{2,1,0:T(2,128)(2,1)S(1)}, u32[]{:S(2)}, u32[]{:S(2)}) collective-permute-start(bf16[3,2,128]{2,1,0:T(2,128)(2,1)S(1)} %pad_maximum_fusion.1), channel_id=1, source_target_pairs={{0,32},{32,64},{64,96},{96,128},{128,160},{160,192},{192,224},{224... | collective-permute-start | bytes 4616 | tf_op jit(solution)/shard_map/ppermute | solution.py:14
  12.9 0.8 fusion.29
  13.8 0.7 convert_element_type.59
  14.4 0.0 collective-permute-done
  14.4 0.9 maximum_convert_fusion
  15.4 0.1 fusion.2
  15.5 0.1 fusion.15
  15.6 62.6 %psum.7 = f32[256]{0:T(256)S(1)} all-reduce(f32[256]{0:T(256)S(1)} %get-tuple-element.10), channel_id=1, replica_groups=mesh['dp'=16,'expert'=32] {'expert'}, use_global_device_ids=true, to_apply=%region_1.0 | all-reduce | flops 256 | bytes 2048 | tf_op jit(solution)/shard_map/psum | solution.py:47
  78.2 0.7 fusion.17
  79.0 0.0 all-gather.3.cloned.1.call-update
  79.0 0.0 all-gather.5.cloned.1.call-start
  79.0 0.7 all-gather.5.cloned.1.call-update
  79.7 0.0 reduce-scatter.2.cloned.1.call-start
  79.8 0.7 pad_maximum_fusion
  80.5 0.7 fusion.24
  81.2 2.8 gather_fusion
  84.0 0.0 copy-done.2
  84.0 2.6 gather_fusion.2
  86.6 0.0 copy-done.3
  86.6 0.2 reduce-window.8
  86.8 0.1 fusion.25
  86.9 81.5 %all-gather.3.cloned.1.call-done = bf16[256,4096]{1,0:T(8,128)(2,1)} async-done(((bf16[256,128]{1,0:T(8,128)(2,1)}), bf16[256,4096]{1,0:T(8,128)(2,1)}) %all-gather.3.cloned.1.call-update) | async-done | bytes 2097168 | tf_op jit(solution)/shard_map/all_gather | solution.py:50
  168.4 1.8 concatenate.14
  170.1 4.1 %gather_fusion.1 = bf16[384,4096]{1,0:T(8,128)(2,1)} fusion(bf16[257,4096]{1,0:T(8,128)(2,1)S(1)} %concatenate.14, s32[1024]{0:T(1024)S(1)} %pad_clamp_fusion), kind=kCustom, calls=%fused_computation.1 | custom fusion | bytes 6292992 | tf_op jit(solution)/shard_map/gather | solution.py:58
  174.2 0.0 copy-start
  174.2 42.7 %all-gather.5.cloned.1.call-done = bf16[4096,2,256]{2,1,0:T(2,128)(2,1)} async-done(((bf16[256,2,256]{2,1,0:T(2,128)(2,1)}), bf16[4096,2,256]{2,1,0:T(2,128)(2,1)}) %all-gather.5.cloned.1.call-update) | async-done | bytes 4194320 | tf_op jit(solution)/shard_map/all_gather | solution.py:67
  217.0 0.0 copy-start.1
  217.0 7.5 %convolution_convert_fusion = bf16[3,4096,256]{2,0,1:T(4,128)(2,1)S(1)} fusion(bf16[4096,2,256]{2,1,0:T(2,128)(2,1)} %all-gather.5.cloned.1.call-done, s32[3]{0:T(128)S(1)} %broadcast_minimum_fusion), kind=kOutput, calls=%fused_computation.5 | convolution fusion | flops 15728646 | bytes 10485772 | tf_op jit(solution)/shard_map/neh,be->bnh/dot_general | solution.py:65
  224.4 0.0 copy-done
  224.5 0.0 copy-done.1
  224.5 1.3 fusion.6
  225.8 4.4 %bitcast_convert_fusion = bf16[4096,2,256]{2,0,1:T(8,128)(2,1)} fusion(bf16[3,128,4096,1]{2,1,0,3:T(8,128)(2,1)S(1)} %bitcast.50, bf16[2,3]{1,0:T(2,128)(2,1)S(1)} %compare_convert_fusion, bf16[3,128,256]{2,1,0:T(8,128)(2,1)S(1)} %get-tuple-element.15), kind=kOutput, calls=%fused_computation.4 | convolution fusion | flops 1613496320 | bytes 7536652 | tf_op jit(solution)/shard_map/brd,ebrh->deh/dot_general | solution.py:89
  230.1 0.0 reduce-scatter.2.cloned.1.call-update
  230.2 0.1 fusion.8
  230.3 1.9 scatter_custom_fusion
  232.2 0.7 slice.56
  232.8 62.2 %reduce-scatter.2.cloned.1.call-done = bf16[256,2,256]{2,0,1:T(8,128)(2,1)} async-done(((bf16[4096,2,256]{2,0,1:T(8,128)(2,1)}), bf16[256,2,256]{2,0,1:T(8,128)(2,1)}) %reduce-scatter.2.cloned.1.call-update) | async-done | bytes 262160 | tf_op jit(solution)/shard_map/reduce_scatter | solution.py:88
  295.1 2.0 copy.21
  (9 shorter events, 0.1 us)
Async XLA Ops:
  7.2 76.8 %copy-start.2 = (bf16[256,256]{1,0:T(8,128)(2,1)S(1)}, bf16[256,256]{1,0:T(8,128)(2,1)}, u32[]{:S(2)}) copy-start(bf16[256,256]{1,0:T(8,128)(2,1)} %param.19) | copy-start | bytes 393220
  7.2 79.4 %copy-start.3 = (s32[1,2]{1,0:T(1,128)S(1)}, s32[1,2]{1,0:T(1,128)}, u32[]{:S(2)}) copy-start(s32[1,2]{1,0:T(1,128)} %param.16) | copy-start | bytes 28
  7.2 161.2 %all-gather.3.cloned.1.call-start = ((), (), s32[]{:S(2)}) async-start(), calls=%async_computation.1 | async-start | bytes 2162688 | tf_op jit(solution)/shard_map/all_gather | solution.py:50
  8.0 6.5 %collective-permute-start = (bf16[3,2,128]{2,1,0:T(2,128)(2,1)S(1)}, bf16[3,2,128]{2,1,0:T(2,128)(2,1)S(1)}, u32[]{:S(2)}, u32[]{:S(2)}) collective-permute-start(bf16[3,2,128]{2,1,0:T(2,128)(2,1)S(1)} %pad_maximum_fusion.1), channel_id=1, source_target_pairs={{0,32},{32,64},{64,96},{96,128},{128,160},{160,192},{192,224},{224... | collective-permute-start | bytes 4616 | tf_op jit(solution)/shard_map/ppermute | solution.py:14
  79.0 138.0 %all-gather.5.cloned.1.call-start = ((), (), s32[]{:S(2)}) async-start(), calls=%async_computation.2 | async-start | bytes 4456448 | tf_op jit(solution)/shard_map/all_gather | solution.py:67
  79.7 215.3 %reduce-scatter.2.cloned.1.call-start = ((), (), s32[]{:S(2)}) async-start(), calls=%async_computation.3 | async-start | bytes 4456448 | tf_op jit(solution)/shard_map/reduce_scatter | solution.py:88
  174.2 50.2 %copy-start = (bf16[384,4096]{1,0:T(8,128)(2,1)S(1)}, bf16[384,4096]{1,0:T(8,128)(2,1)}, u32[]{:S(2)}) copy-start(bf16[384,4096]{1,0:T(8,128)(2,1)} %gather_fusion.1) | copy-start | bytes 9437188
  217.0 7.5 %copy-start.1 = (bf16[384,256]{1,0:T(8,128)(2,1)S(1)}, bf16[384,256]{1,0:T(8,128)(2,1)}, u32[]{:S(2)}) copy-start(bf16[384,256]{1,0:T(8,128)(2,1)} %gather_fusion.2) | copy-start | bytes 589828
Sparse Core Ops, SparseCore 0:
  79.1 89.2 all-gather.2
  170.5 46.4 all-gather.4
  230.3 64.7 reduce-scatter.1
where the time goes:
time: 304 us
  waiting for transfers between devices  187 us (62%)
  blocking collectives  62.6 us (21%)
  local copies, waits for them, and re-layouts  16.6 us (5%)
  between operations  13.9 us (5%)
  matrix products  13.1 us (4%)
  other arithmetic  5.15 us (2%)
  starting transfers between devices  5.08 us (2%)
    all_gather x1, waiting for transfers between devices, on_device(): gathered = lax.all_gather(normed, 'expert', axis=1, tiled=True)  81.5 us
    psum x1, blocking collectives, on_device(): total = lax.psum(jnp.sum(mixed_f * mixed_f, axis=1), 'expert')  62.6 us
    reduce_scatter x1, waiting for transfers between devices, on_device(): lax.psum_scatter(jnp.einsum('brd,ebrh->deh', columns, masked_grad, prefer...  62.2 us
    all_gather x1, waiting for transfers between devices, on_device(): lax.all_gather(w_proj, 'dp', axis=0, tiled=True)  42.7 us
    dot_general x1, matrix products, on_device(): jnp.einsum('neh,be->bnh', lax.all_gather(w_proj, 'dp', axis=0, tiled=True...  7.48 us
  transfers between devices with their start and end apart: 4, of which 3 were waited for; matrix products, arithmetic and copies ran while one was open for 6% of the time, Pallas kernels for 0%

commit v1 on v0

--- a/solution.py
+++ b/solution.py
@@ -64,7 +64,9 @@
     columns = x_blocks
     chosen_w = jnp.einsum(
         "neh,be->bnh",
-        lax.all_gather(w_proj, "dp", axis=0, tiled=True),
+        jnp.concatenate(
+            lax.all_to_all(jnp.stack([w_proj] * lax.axis_size("dp")), "dp", 0, 0), axis=0
+        ),
         selector,
         preferred_element_type=jnp.float32,
     ).astype(jnp.bfloat16)

time: 304 us -> 362 us (1.19)
  the two profiles are of different devices: /device:TPU:29 before, /device:TPU:25 now
where the time goes in v1:
time: 362 us; the launch traced here: 361 us
  waiting for transfers between devices  231 us (64%)
  blocking collectives  64.5 us (18%)
  local copies, waits for them, and re-layouts  21.5 us (6%)
  starting transfers between devices  15.2 us (4%)
  between operations  14.3 us (4%)
  matrix products  13.3 us (4%)
    ppermute x1, waiting for transfers between devices, from_behind(): lax.ppermute(value, axis, [(source, source + steps) for source in range(l...  85.9 us
    all_gather x1, waiting for transfers between devices, on_device(): gathered = lax.all_gather(normed, 'expert', axis=1, tiled=True)  80.3 us
    reduce_scatter x1, waiting for transfers between devices, on_device(): lax.psum_scatter(jnp.einsum('brd,ebrh->deh', columns, masked_grad, prefer...  65 us
    psum x1, blocking collectives, on_device(): total = lax.psum(jnp.sum(mixed_f * mixed_f, axis=1), 'expert')  64.5 us
    all_to_all x1, starting transfers between devices, on_device(): lax.all_to_all(jnp.stack([w_proj] * lax.axis_size('dp')), 'dp', 0, 0)  10.3 us
    dot_general x1, matrix products, on_device(): jnp.einsum('neh,be->bnh', jnp.concatenate(lax.all_to_all(jnp.stack([w_pro...  7.6 us
  transfers between devices with their start and end apart: 4, of which 3 were waited for; matrix products, arithmetic and copies ran while one was open for 4% of the time, Pallas kernels for 0%

profile of v1, /device:TPU:25, one launch (start us, length us, event | category | flops | bytes accessed | tf_op | source)
XLA Modules:
  0.0 361.4 jit_solution(1844329088786999391)
XLA Ops:
  7.2 6.2 %stack.14 = bf16[16,256,2,256]{3,2,1,0:T(2,128)(2,1)} broadcast(bf16[256,2,256]{2,1,0:T(2,128)(2,1)} %param.18), dimensions={1,2,3} | broadcast | bytes 4456448 | tf_op jit(solution)/shard_map/stack | solution.py:68
  13.3 0.0 copy-start.1
  13.3 0.0 copy-start.2
  13.3 0.0 copy-start.3
  13.3 0.0 copy-start.5
  13.3 0.0 copy-start.8
  13.3 0.0 copy-start.7
  13.4 0.0 copy-start.6
  13.4 10.3 %all-to-all-start = ((bf16[16,256,2,256]{3,2,1,0:T(2,128)(2,1)}), bf16[16,256,2,256]{3,2,1,0:T(2,128)(2,1)}, u32[]{:S(2)}, u32[]{:S(2)}) async-start(bf16[16,256,2,256]{3,2,1,0:T(2,128)(2,1)} %stack.14), calls=%async_computation | async-start | bytes 8388608 | tf_op jit(solution)/shard_map/all_to_all | solution.py:68
  23.7 0.0 copy-start.4
  23.7 0.0 copy-start.9
  23.7 0.0 all-gather.2.cloned.1.call-start
  23.8 0.0 copy-done.1
  23.8 0.0 copy-done.2
  23.8 0.0 copy-done.3
  23.8 4.6 %collective-permute-start = (bf16[3,2,128]{2,1,0:T(2,128)(2,1)S(1)}, bf16[3,2,128]{2,1,0:T(2,128)(2,1)S(1)}, u32[]{:S(2)}, u32[]{:S(2)}) collective-permute-start(bf16[3,2,128]{2,1,0:T(2,128)(2,1)S(1)} %pad_maximum_fusion.1), channel_id=1, source_target_pairs={{0,32},{32,64},{64,96},{96,128},{128,160},{160,192},{192,224},{224... | collective-permute-start | bytes 4616 | tf_op jit(solution)/shard_map/ppermute | solution.py:14
  28.4 0.0 copy-done.5
  28.4 0.0 copy-done.8
  28.5 85.9 %collective-permute-done = bf16[3,2,128]{2,1,0:T(2,128)(2,1)S(1)} collective-permute-done((bf16[3,2,128]{2,1,0:T(2,128)(2,1)S(1)}, bf16[3,2,128]{2,1,0:T(2,128)(2,1)S(1)}, u32[]{:S(2)}, u32[]{:S(2)}) %collective-permute-start) | collective-permute-done | bytes 1568 | tf_op jit(solution)/shard_map/ppermute | solution.py:14
  114.4 0.1 fusion.2
  114.5 0.1 fusion.15
  114.6 64.5 %psum.7 = f32[256]{0:T(256)S(1)} all-reduce(f32[256]{0:T(256)S(1)} %get-tuple-element.8), channel_id=1, replica_groups=mesh['dp'=16,'expert'=32] {'expert'}, use_global_device_ids=true, to_apply=%region_1.0 | all-reduce | flops 256 | bytes 2048 | tf_op jit(solution)/shard_map/psum | solution.py:47
  179.1 0.7 fusion.17
  179.8 0.0 all-gather.2.cloned.1.call-update
  179.9 0.2 reduce-scatter.2.cloned.1.call-start
  180.1 0.0 copy-done.7
  180.1 0.0 copy-done.6
  180.2 2.8 gather_fusion
  183.0 0.0 copy-done.4
  183.0 2.1 gather_fusion.2
  185.1 0.0 copy-done.9
  185.1 0.2 reduce-window.8
  185.3 0.1 fusion.25
  185.4 80.3 %all-gather.2.cloned.1.call-done = bf16[256,4096]{1,0:T(8,128)(2,1)} async-done(((bf16[256,128]{1,0:T(8,128)(2,1)}), bf16[256,4096]{1,0:T(8,128)(2,1)}) %all-gather.2.cloned.1.call-update) | async-done | bytes 2097168 | tf_op jit(solution)/shard_map/all_gather | solution.py:50
  265.7 1.8 concatenate.14
  267.5 4.0 %gather_fusion.1 = bf16[384,4096]{1,0:T(8,128)(2,1)} fusion(bf16[257,4096]{1,0:T(8,128)(2,1)S(1)} %concatenate.14, s32[1024]{0:T(1024)S(1)} %pad_clamp_fusion), kind=kCustom, calls=%fused_computation.1 | custom fusion | bytes 6292992 | tf_op jit(solution)/shard_map/gather | solution.py:58
  271.5 0.0 all-to-all-done
  271.5 0.0 copy-start
  271.5 7.6 %convolution_convert_fusion = bf16[3,4096,256]{2,0,1:T(4,128)(2,1)S(1)} fusion(bf16[4096,2,256]{2,1,0:T(2,128)(2,1)} %bitcast.10, s32[3]{0:T(128)S(1)} %broadcast_minimum_fusion), kind=kOutput, calls=%fused_computation.5 | convolution fusion | flops 15728646 | bytes 10485772 | tf_op jit(solution)/shard_map/neh,be->bnh/dot_general | solution.py:65
  279.1 0.0 copy-done
  279.2 1.3 fusion.6
  280.4 4.4 %bitcast_convert_fusion = bf16[4096,2,256]{2,0,1:T(8,128)(2,1)} fusion(bf16[3,128,4096,1]{2,1,0,3:T(8,128)(2,1)S(1)} %bitcast.51, bf16[2,3]{1,0:T(2,128)(2,1)S(1)} %compare_convert_fusion, bf16[3,128,256]{2,1,0:T(8,128)(2,1)S(1)} %get-tuple-element.13), kind=kOutput, calls=%fused_computation.4 | convolution fusion | flops 1613496320 | bytes 7536652 | tf_op jit(solution)/shard_map/brd,ebrh->deh/dot_general | solution.py:91
  284.9 0.0 reduce-scatter.2.cloned.1.call-update
  284.9 0.1 fusion.8
  285.0 1.9 scatter_custom_fusion
  286.9 0.7 slice.56
  287.6 65.0 %reduce-scatter.2.cloned.1.call-done = bf16[256,2,256]{2,0,1:T(8,128)(2,1)} async-done(((bf16[4096,2,256]{2,0,1:T(8,128)(2,1)}), bf16[256,2,256]{2,0,1:T(8,128)(2,1)}) %reduce-scatter.2.cloned.1.call-update) | async-done | bytes 262160 | tf_op jit(solution)/shard_map/reduce_scatter | solution.py:90
  352.6 2.0 copy.18
  (15 shorter events, 0.2 us)
Async XLA Ops:
  13.3 10.5 %copy-start.1 = (bf16[256,128]{1,0:T(8,128)(2,1)S(1)}, bf16[256,128]{1,0:T(8,128)(2,1)}, u32[]{:S(2)}) copy-start(bf16[256,128]{1,0:T(8,128)(2,1)} %param.12) | copy-start | bytes 196612
  13.3 10.5 %copy-start.2 = (bf16[256,128]{1,0:T(8,128)(2,1)S(1)}, bf16[256,128]{1,0:T(8,128)(2,1)}, u32[]{:S(2)}) copy-start(bf16[256,128]{1,0:T(8,128)(2,1)} %param.11) | copy-start | bytes 196612
  13.3 10.5 %copy-start.3 = (bf16[256,128]{1,0:T(8,128)(2,1)S(1)}, bf16[256,128]{1,0:T(8,128)(2,1)}, u32[]{:S(2)}) copy-start(bf16[256,128]{1,0:T(8,128)(2,1)} %param.10) | copy-start | bytes 196612
  13.3 15.1 %copy-start.5 = (f32[3,3,128]{2,1,0:T(4,128)S(1)}, f32[3,3,128]{2,1,0:T(4,128)}, u32[]{:S(2)}) copy-start(f32[3,3,128]{2,1,0:T(4,128)} %param.13) | copy-start | bytes 13828
  13.3 15.1 %copy-start.8 = (bf16[128]{0:T(256)(128)(2,1)S(1)}, bf16[128]{0:T(256)(128)(2,1)}, u32[]{:S(2)}) copy-start(bf16[128]{0:T(256)(128)(2,1)} %param.14) | copy-start | bytes 772
  13.3 166.8 %copy-start.7 = (f32[256]{0:T(256)S(1)}, f32[256]{0:T(256)}, u32[]{:S(2)}) copy-start(f32[256]{0:T(256)} %param.17) | copy-start | bytes 3076
  13.4 166.8 %copy-start.6 = (s32[1,384]{1,0:T(1,128)S(1)}, s32[1,384]{1,0:T(1,128)}, u32[]{:S(2)}) copy-start(s32[1,384]{1,0:T(1,128)} %param.15) | copy-start | bytes 4612
  13.4 258.2 %all-to-all-start = ((bf16[16,256,2,256]{3,2,1,0:T(2,128)(2,1)}), bf16[16,256,2,256]{3,2,1,0:T(2,128)(2,1)}, u32[]{:S(2)}, u32[]{:S(2)}) async-start(bf16[16,256,2,256]{3,2,1,0:T(2,128)(2,1)} %stack.14), calls=%async_computation | async-start | bytes 8388608 | tf_op jit(solution)/shard_map/all_to_all | solution.py:68
  23.7 159.3 %copy-start.4 = (bf16[256,256]{1,0:T(8,128)(2,1)S(1)}, bf16[256,256]{1,0:T(8,128)(2,1)}, u32[]{:S(2)}) copy-start(bf16[256,256]{1,0:T(8,128)(2,1)} %param.19) | copy-start | bytes 393220
  23.7 161.3 %copy-start.9 = (s32[1,2]{1,0:T(1,128)S(1)}, s32[1,2]{1,0:T(1,128)}, u32[]{:S(2)}) copy-start(s32[1,2]{1,0:T(1,128)} %param.16) | copy-start | bytes 28
  23.7 242.0 %all-gather.2.cloned.1.call-start = ((), (), s32[]{:S(2)}) async-start(), calls=%async_computation.2 | async-start | bytes 2162688 | tf_op jit(solution)/shard_map/all_gather | solution.py:50
  23.8 90.5 %collective-permute-start = (bf16[3,2,128]{2,1,0:T(2,128)(2,1)S(1)}, bf16[3,2,128]{2,1,0:T(2,128)(2,1)S(1)}, u32[]{:S(2)}, u32[]{:S(2)}) collective-permute-start(bf16[3,2,128]{2,1,0:T(2,128)(2,1)S(1)} %pad_maximum_fusion.1), channel_id=1, source_target_pairs={{0,32},{32,64},{64,96},{96,128},{128,160},{160,192},{192,224},{224... | collective-permute-start | bytes 4616 | tf_op jit(solution)/shard_map/ppermute | solution.py:14
  179.9 172.7 %reduce-scatter.2.cloned.1.call-start = ((), (), s32[]{:S(2)}) async-start(), calls=%async_computation.3 | async-start | bytes 4456448 | tf_op jit(solution)/shard_map/reduce_scatter | solution.py:90
  271.5 7.6 %copy-start = (bf16[384,4096]{1,0:T(8,128)(2,1)S(1)}, bf16[384,4096]{1,0:T(8,128)(2,1)}, u32[]{:S(2)}) copy-start(bf16[384,4096]{1,0:T(8,128)(2,1)} %gather_fusion.1) | copy-start | bytes 9437188
Sparse Core Ops, SparseCore 0:
  180.0 85.6 all-gather.1
  285.0 67.5 reduce-scatter.1
